TPU v7x, 32 devices: a whole 2x2x4 slice. The times are simulated.
32 devices in a mesh: prow: 8 (over z, y), pcol: 4 (over x, core).
Axes of the slice: x: 2, y: 2, z: 4, core: 2. Of those that a mesh axis runs over, the one named last changes fastest.
Arguments:
- data: float32 [16384, 8192], P('prow', 'pcol'), may hold values from 0.05 to 5
- w_trans: float32 [32, 16384], P(None, ('prow', 'pcol')), as said below
- h_prior: float32 [32, 8192], P(None, 'pcol'), may hold values from 0.1 to 3
Outputs:
- h_next: float32 [32, 8192], P(None, 'pcol')
Inputs may be any that keep to these rules, and one draw needn't show every extreme that they name: `w_trans`: every entry is positive.
All inputs are finite; a program needn't handle non-finite values.
Results may differ from a plain program's by a relative error of at most 0.0003.
Values sent between devices are 32-bit elements; how exact they have to be, the bound alone decides.
No kernel may reach another device: no remote copies, remote signals or barrier semaphores. Data moves between devices by JAX's collectives and lax.ppermute only.
A program may use at most 64 MiB of HBM per device.

v0:
```python
import functools

import jax
import jax.numpy as jnp
from jax import lax
from jax.experimental import pallas as pl
from jax.experimental.pallas import tpu as pltpu
from jax.sharding import PartitionSpec as P

LANES = 128
GRAM_ROWS = 8
VMEM = pl.BlockSpec(memory_space=pltpu.VMEM)
HBM = pl.BlockSpec(memory_space=pltpu.HBM)


def call(kernel, out_shape, operands, name, mebibytes=4, in_specs=None, scratch=(), cost=None,
         out_specs=VMEM):
    many = isinstance(out_shape, list)
    return pl.pallas_call(
        kernel,
        out_shape=out_shape,
        in_specs=in_specs or [VMEM] * len(operands),
        out_specs=[out_specs] * len(out_shape) if many else out_specs,
        compiler_params=pltpu.CompilerParams(vmem_limit_bytes=mebibytes * 1024 * 1024),
        scratch_shapes=list(scratch),
        cost_estimate=cost,
        name=name,
    )(*operands)


def floats(*shape):
    return jax.ShapeDtypeStruct(shape, jnp.float32)


def split(value):
    high = value.astype(jnp.bfloat16)
    low = (value - high.astype(jnp.float32)).astype(jnp.bfloat16)
    return high, low


def exact_dot(left, right, dims):
    return lax.dot_general(
        left, right, (dims, ((), ())),
        precision=lax.Precision.HIGHEST, preferred_element_type=jnp.float32,
    )


def block_start(near, width, side_turn, level_turn):
    row_at = lax.axis_index("prow")
    side, level = lax.rem(row_at, near), lax.div(row_at, near)
    peer = (level ^ level_turn) * near + (side ^ side_turn)
    return pl.multiple_of(peer * width, width)


def row_part(depth, turn):
    return pl.ds(pl.multiple_of((lax.axis_index("pcol") ^ turn) * depth, depth), depth)


def block_copies(near, width, n_col, order, data_ref, out_ref, sems):
    depth = data_ref.shape[0] // n_col
    copies = {}
    for (at, turns), turn in order:
        columns = pl.ds(block_start(near, width, *turns), width)
        rows = row_part(depth, turn)
        copies[at, turn] = pltpu.make_async_copy(
            data_ref.at[rows, columns], out_ref.at[at, rows], sems.at[at, turn]
        )
    return copies


def split_basis(part_ref, out_ref, turn):
    rank = part_ref.shape[0]
    part = part_ref[...]
    high, low = split(part)
    out_ref[turn, :rank] = high
    out_ref[turn, rank:] = low
    return exact_dot(part, part, ((1,), (1,)))


def product(w_split, blocks, at, turns):
    rank, depth = w_split.shape[1] // 2, w_split.shape[2]
    total = None
    for turn in turns:
        high, low = split(blocks[at, row_part(depth, turn)])
        upper = jnp.dot(w_split[turn], high, preferred_element_type=jnp.float32)
        term = (
            upper[:rank]
            + upper[rank:]
            + jnp.dot(w_split[turn, :rank], low, preferred_element_type=jnp.float32)
        )
        total = term if total is None else total + term
    return total


def store(cross, out_ref, row, before=None):
    rank = cross.shape[0]
    for i in range(cross.shape[1] // LANES):
        rows = slice(row + rank * i, row + rank * (i + 1))
        piece = cross[:, LANES * i : LANES * (i + 1)]
        out_ref[rows] = piece if before is None else piece + before[rows]


def own_region(compute):
    pl.when(lax.axis_index("prow") >= 0)(compute)


def load_kernel(near, width, n_col, early, late, others, *refs):
    w_refs, data_ref = refs[: len(early)], refs[len(early)]
    blocks, begun, w_split, gram_ref, sems = refs[len(early) + 1 :]
    order = [(at, turn) for turn in early + late for at in enumerate(others)]
    copies = block_copies(near, width, n_col, order, data_ref, blocks, sems)
    for copy in copies.values():
        copy.start()

    def compute():
        gram = split_basis(w_refs[0], w_split, early[0])
        for turn, ref in list(zip(early, w_refs))[1:]:
            gram = gram + split_basis(ref, w_split, turn)
        gram_ref[...] = gram
        for at in range(len(others)):
            for turn in early:
                copies[at, turn].wait()
            store(product(w_split, blocks, at, early), begun.at[at], 0)

    own_region(compute)
    for (_, turn), copy in copies.items():
        if turn not in early:
            copy.wait()


def other_side_kernel(near, width, n_col, slab, far, early, late, own, fetched, *refs):
    w_refs, (w_early, gram_early, blocks, begun, data_ref) = refs[: len(late)], refs[len(late) :][:5]
    *out_refs, w_split, gram_ref, own_block, sems = refs[len(late) + 5 :]
    rank = w_refs[0].shape[0]
    order = [((0, own), turn) for turn in fetched]
    copies = block_copies(near, width, n_col, order, data_ref, own_block, sems)
    for copy in copies.values():
        copy.start()

    def compute():
        for turn in early:
            w_split[turn] = w_early[turn]
        gram = gram_early[...]
        for turn, ref in zip(late, w_refs):
            gram = gram + split_basis(ref, w_split, turn)
        slabs = [gram[GRAM_ROWS * i : GRAM_ROWS * (i + 1)] for i in range(rank // GRAM_ROWS)]
        packed = jnp.concatenate(slabs, axis=1)
        gram_ref[...] = packed
        for index, out_ref in enumerate(out_refs):
            for at in range(far):
                block = index * far + at
                store(
                    product(w_split, blocks, block, late), out_ref.at[pl.ds(slab * at, slab)], 0,
                    begun.at[block],
                )
            out_ref[slab * far :] = packed

    own_region(compute)
    for copy in copies.values():
        copy.wait()


def own_side_kernel(near, width, n_col, owns, fetched, w_split, first_rows, data_ref, *refs):
    out_ref, blocks, sems = refs
    order = [(at, turn) for at in enumerate(owns) for turn in range(n_col)]
    order = [(at, turn) for at, turn in order if at[0] or turn not in fetched]
    copies = block_copies(near, width, n_col, order, data_ref, blocks, sems)
    for copy in copies.values():
        copy.start()

    def multiply(at):
        total = None if at else product(w_split, first_rows, 0, fetched)
        for turn in range(n_col):
            if (at, turn) in copies:
                copies[at, turn].wait()
                term = product(w_split, blocks, at, [turn])
                total = term if total is None else total + term
        store(total, out_ref.at[at], 0)

    for at in range(len(owns)):
        own_region(functools.partial(multiply, at))


def side_sum_kernel(slab, turns, pairs, own_ref, gram_ref, *refs):
    got_refs, out_refs = refs[: -len(pairs)], refs[-len(pairs) :]
    gram = gram_ref[...]
    for got in got_refs:
        gram = gram + got[slab * len(turns) :]
    for pair, out_ref in zip(pairs, out_refs):
        for at, turn in enumerate(pair):
            place = turns.index(turn)
            total = own_ref[place]
            for got in got_refs:
                total = total + got[slab * place : slab * (place + 1)]
            out_ref[slab * at : slab * (at + 1)] = total
        out_ref[slab * len(pair) :] = gram


def peer_start(near, width, level, side):
    return pl.multiple_of((level * near + side) * width, width)


def sweep_kernel(near, width, *refs):
    parts, h_ref, out_ref = refs[:-2], refs[-2], refs[-1]
    rank = h_ref.shape[0]
    row_at = lax.axis_index("prow")
    side, level = lax.rem(row_at, near), lax.div(row_at, near)
    pieces = width // LANES
    slab = rank * pieces
    packed, chunks = None, [None, None]
    for part in parts:
        gram_part = part[2 * slab :]
        packed = gram_part if packed is None else packed + gram_part
        for at in range(2):
            piece = part[slab * at : slab * (at + 1)]
            chunks[at] = piece if chunks[at] is None else chunks[at] + piece
    cross = jnp.concatenate(
        [chunk[rank * i : rank * (i + 1)] for chunk in chunks for i in range(pieces)], axis=1
    )
    gram = jnp.concatenate(
        [packed[:, rank * i : rank * (i + 1)] for i in range(rank // GRAM_ROWS)], axis=0
    )
    starts = [peer_start(near, width, at, side) for at in (level, level ^ 2)]
    h = jnp.concatenate([h_ref[:, pl.ds(start, width)] for start in starts], axis=1)
    rest = cross - exact_dot(gram, h, ((1,), (0,)))
    rows = []
    for k in range(rank):
        inverse = 1.0 / gram[k : k + 1, k : k + 1]
        old = h[k : k + 1]
        fresh = jnp.maximum(old + rest[k : k + 1] * inverse, 0.0)
        rows.append(fresh)
        rest = rest - gram[:, k : k + 1] * (fresh - old)
    done = jnp.concatenate(rows, axis=0)
    for at in range(2):
        out_ref[at] = done[:, width * at : width * (at + 1)]


def assemble_kernel(near, width, members, *refs):
    piece_refs, (out_ref, sems) = refs[:-2], refs[-2:]
    row_at = lax.axis_index("prow")
    side, level = lax.rem(row_at, near), lax.div(row_at, near)
    copies = []
    for member, ((above, side_turn), piece_ref) in enumerate(zip(members, piece_refs)):
        theirs = level ^ above
        for at, source in enumerate((theirs, theirs ^ 2)):
            columns = pl.ds(peer_start(near, width, source, side ^ side_turn), width)
            copy = pltpu.make_async_copy(
                piece_ref.at[at], out_ref.at[:, columns], sems.at[member, at]
            )
            copy.start()
            copies.append(copy)
    for copy in copies:
        copy.wait()


def shards(n_row, n_col, data, w_trans, h_prior):
    rank, depth = w_trans.shape
    rows, cols = data.shape
    width = cols // n_row
    near = max(1, n_row // 4)
    far = n_row // near
    slab = rank * (width // LANES)
    turns = [*range(far // 2, far), *range(far // 2 - 1, -1, -1)]
    sides = range(1, near)

    def permute(value, axis, turn):
        size = n_row if axis == "prow" else n_col
        return lax.ppermute(value, axis, [(i, i ^ turn) for i in range(size)])

    w_parts = [w_trans] + [permute(w_trans, "pcol", t) for t in range(1, n_col)]
    early = list(range(1, min(2, n_col)))
    late = [turn for turn in range(n_col) if turn not in early]
    others = [(side, turn) for side in sides for turn in turns]
    owns = [(0, turn) for turn in turns]
    split_parts = jax.ShapeDtypeStruct((n_col, 2 * rank, depth), jnp.bfloat16)
    blocks, begun, w_early, gram_early = call(
        functools.partial(load_kernel, near, width, n_col, early, late, others),
        [
            floats(len(others), rows, width),
            floats(len(others), slab, LANES),
            split_parts,
            floats(rank, rank),
        ],
        [*(w_parts[t] for t in early), data], "load_other_side", 40,
        [VMEM] * len(early) + [HBM], [pltpu.SemaphoreType.DMA((len(others), n_col))],
        pl.CostEstimate(
            flops=0, bytes_accessed=8 * rows * width * len(others), transcendentals=0
        ),
    )
    fetched = list(range(n_col // 2))
    *sent, w_split, gram, own_block = call(
        functools.partial(
            other_side_kernel, near, width, n_col, slab, far, early, late, owns[0], fetched
        ),
        [floats(far * slab + GRAM_ROWS, LANES)] * len(sides)
        + [split_parts, floats(GRAM_ROWS, LANES), floats(1, rows, width)],
        [*(w_parts[t] for t in late), w_early, gram_early, blocks, begun, data], "other_side", 37,
        [VMEM] * (len(late) + 4) + [HBM], [pltpu.SemaphoreType.DMA((1, n_col))],
    )
    got = [permute(sent[side - 1], "prow", side) for side in sides]
    own = call(
        functools.partial(own_side_kernel, near, width, n_col, owns, fetched),
        floats(far, slab, LANES), [w_split, own_block, data], "own_side", 40,
        [VMEM] * 2 + [HBM],
        [
            pltpu.VMEM((far, rows, width), jnp.float32),
            pltpu.SemaphoreType.DMA((far, n_col)),
        ],
    )
    pairs = [(2, 0), (3, 1), (1, 3), (0, 2)]
    sums = call(
        functools.partial(side_sum_kernel, slab, turns, pairs),
        [floats(2 * slab + GRAM_ROWS, LANES)] * len(pairs), [own, gram, *got], "side_sum",
    )
    parts = [
        permute(value, "prow", pair[0] * near) if pair[0] else value
        for pair, value in zip(pairs, sums)
    ]
    fresh = call(
        functools.partial(sweep_kernel, near, width), floats(2, rank, width), [*parts, h_prior],
        "row_sweep",
    )
    members = [(0, 0), (1, 0)] + [(above, side) for above in range(2) for side in sides]
    pieces = [
        permute(fresh, "prow", above * near + side) if above or side else fresh
        for above, side in members
    ]
    return call(
        functools.partial(assemble_kernel, near, width, members), floats(rank, cols), pieces,
        "assemble", scratch=[pltpu.SemaphoreType.DMA((len(members), 2))], out_specs=HBM,
    )


def solution(mesh):
    n_row, n_col = mesh.shape["prow"], mesh.shape["pcol"]
    placed = (P("prow", "pcol"), P(None, ("prow", "pcol")), P(None, "pcol"))
    return jax.shard_map(
        functools.partial(shards, n_row, n_col),
        mesh=mesh, in_specs=placed, out_specs=P(None, "pcol"), check_vma=False,
    )
```

profile of v0, /device:TPU:0, one launch (start us, length us, event | category | flops | bytes accessed | tf_op | source)
XLA Modules:
  0.0 31.1 jit_solution(15289458539873464545)
XLA Ops:
  0.0 0.0 copy-start.1
  0.0 0.5 %collective-permute-start.2 = (f32[32,512]{1,0:T(8,128)}, f32[32,512]{1,0:T(8,128)S(1)}, u32[]{:S(2)}, u32[]{:S(2)}) collective-permute-start(f32[32,512]{1,0:T(8,128)} %refs_0_.1), channel_id=1, source_target_pairs={{0,1},{1,0},{2,3},{3,2},{4,5},{5,4},{6,7},{7,6},{8,9},{9,8},{10,11... | collective-permute-start | bytes 196616 | tf_op jit(solution)/shard_map/ppermute | solution.py:268
  0.5 2.6 %collective-permute-start.1 = (f32[32,512]{1,0:T(8,128)}, f32[32,512]{1,0:T(8,128)S(1)}, u32[]{:S(2)}, u32[]{:S(2)}) collective-permute-start(f32[32,512]{1,0:T(8,128)} %refs_0_.1), channel_id=1, source_target_pairs={{0,3},{1,2},{2,1},{3,0},{4,7},{5,6},{6,5},{7,4},{8,11},{9,10},{10,... | collective-permute-start | bytes 196616 | tf_op jit(solution)/shard_map/ppermute | solution.py:268
  3.1 0.1 collective-permute-start
  3.1 0.0 collective-permute-done.2.refs_0_
  3.1 3.7 %load_other_side.1 = (f32[4,2048,256]{2,1,0:T(8,128)S(1)}, f32[4,64,128]{2,1,0:T(8,128)S(1)}, bf16[4,64,512]{2,1,0:T(8,128)(2,1)S(1)}, f32[32,32]{1,0:T(8,128)S(1)}) custom-call(f32[32,512]{1,0:T(8,128)S(1)} %collective-permute-done.2.refs_0_, f32[2048,2048]{1,0:T(8,128)} %data_ref.1), custom_call_target="tpu_custom_call" | custom-call | bytes 16777216 | tf_op jit(solution)/shard_map/load_other_side/pallas_call | solution.py:19
  6.8 0.0 collective-permute-done.1.refs_2_
  6.8 0.7 %collective-permute-done.refs_1_ = f32[32,512]{1,0:T(8,128)S(1)} collective-permute-done((f32[32,512]{1,0:T(8,128)}, f32[32,512]{1,0:T(8,128)S(1)}, u32[]{:S(2)}, u32[]{:S(2)}) %collective-permute-start) | collective-permute-done | bytes 65568 | tf_op jit(solution)/shard_map/ppermute | solution.py:268
  7.5 0.0 copy-done.1
  7.5 1.4 %other_side.1 = (f32[264,128]{1,0:T(8,128)S(1)}, bf16[4,64,512]{2,1,0:T(8,128)(2,1)S(1)}, f32[8,128]{1,0:T(8,128)S(1)}, f32[1,2048,256]{2,1,0:T(8,128)S(1)}) custom-call(f32[32,512]{1,0:T(8,128)S(1)} %copy-done.1, f32[32,512]{1,0:T(8,128)S(1)} %collective-permute-done.refs_1_, f32[32,512]{1,0:T(8,128)S(1)} %collective-permute-done.1.refs_2_, ...), custom_call_target="tpu_custom_call" | custom-call | tf_op jit(solution)/shard_map/other_side/pallas_call | solution.py:19
  9.0 1.6 %collective-permute-start.3 = (f32[264,128]{1,0:T(8,128)S(1)}, f32[264,128]{1,0:T(8,128)S(1)}, u32[]{:S(2)}, u32[]{:S(2)}) collective-permute-start(f32[264,128]{1,0:T(8,128)S(1)} %get-tuple-element.24), channel_id=1, source_target_pairs={{0,4},{4,0},{8,12},{12,8},{16,20},{20,16},{24,28},{28,24},{1,5},{5... | collective-permute-start | bytes 405512 | tf_op jit(solution)/shard_map/ppermute | solution.py:268
  10.6 0.0 copy-start
  10.6 3.8 %own_side.1.own_ref = f32[4,64,128]{2,1,0:T(8,128)S(1)} custom-call(bf16[4,64,512]{2,1,0:T(8,128)(2,1)S(1)} %get-tuple-element.21.w_split, f32[1,2048,256]{2,1,0:T(8,128)S(1)} %get-tuple-element.22.first_rows, f32[2048,2048]{1,0:T(8,128)} %data_ref.1), custom_call_target="tpu_custom_call" | custom-call | tf_op jit(solution)/shard_map/own_side/pallas_call | solution.py:19
  14.4 0.0 collective-permute-done.3.refs_0_
  14.4 2.7 %collective-permute-start.4 = (f32[136,128]{1,0:T(8,128)S(1)}, f32[136,128]{1,0:T(8,128)S(1)}, u32[]{:S(2)}, u32[]{:S(2)}) collective-permute-start(f32[136,128]{1,0:T(8,128)S(1)} %get-tuple-element.25), channel_id=1, source_target_pairs={{0,16},{4,20},{8,24},{12,28},{16,0},{20,4},{24,8},{28,12},{1,17},{... | collective-permute-start | bytes 208904 | tf_op jit(solution)/shard_map/ppermute | solution.py:268
  17.1 1.3 %collective-permute-start.5 = (f32[136,128]{1,0:T(8,128)S(1)}, f32[136,128]{1,0:T(8,128)S(1)}, u32[]{:S(2)}, u32[]{:S(2)}) collective-permute-start(f32[136,128]{1,0:T(8,128)S(1)} %get-tuple-element.26), channel_id=1, source_target_pairs={{0,24},{4,28},{8,16},{12,20},{16,8},{20,12},{24,0},{28,4},{1,25},{... | collective-permute-start | bytes 208904 | tf_op jit(solution)/shard_map/ppermute | solution.py:268
  18.4 0.2 collective-permute-start.6
  18.6 1.2 %collective-permute-done.4.refs_0_ = f32[136,128]{1,0:T(8,128)S(1)} collective-permute-done((f32[136,128]{1,0:T(8,128)S(1)}, f32[136,128]{1,0:T(8,128)S(1)}, u32[]{:S(2)}, u32[]{:S(2)}) %collective-permute-start.4) | collective-permute-done | bytes 69664 | tf_op jit(solution)/shard_map/ppermute | solution.py:268
  19.9 3.5 %collective-permute-done.5.refs_1_ = f32[136,128]{1,0:T(8,128)S(1)} collective-permute-done((f32[136,128]{1,0:T(8,128)S(1)}, f32[136,128]{1,0:T(8,128)S(1)}, u32[]{:S(2)}, u32[]{:S(2)}) %collective-permute-start.5) | collective-permute-done | bytes 69664 | tf_op jit(solution)/shard_map/ppermute | solution.py:268
  23.3 0.1 collective-permute-done.6.refs_2_
  23.5 0.0 copy-done
  23.5 0.5 %row_sweep.1.refs_0_ = f32[2,32,256]{2,1,0:T(8,128)S(1)} custom-call(f32[136,128]{1,0:T(8,128)S(1)} %collective-permute-done.4.refs_0_, f32[136,128]{1,0:T(8,128)S(1)} %collective-permute-done.5.refs_1_, f32[136,128]{1,0:T(8,128)S(1)} %collective-permute-done.6.refs_2_, f32[136,128]{1,0:T(8,128)S(1)} %get-tuple-element.28.refs_3_, f32[32,2048]{1,0:T(8,128)S(1)} %copy-done), custom_call_target="tpu_custom_call" | custom-call | tf_op jit(solution)/shard_map/row_sweep/pallas_call | solution.py:19
  24.0 1.2 %collective-permute-start.9 = (f32[2,32,256]{2,1,0:T(8,128)S(1)}, f32[2,32,256]{2,1,0:T(8,128)S(1)}, u32[]{:S(2)}, u32[]{:S(2)}) collective-permute-start(f32[2,32,256]{2,1,0:T(8,128)S(1)} %row_sweep.1.refs_0_), channel_id=1, source_target_pairs={{0,12},{4,8},{8,4},{12,0},{16,28},{20,24},{24,20},{28,16},{1,13},{... | collective-permute-start | bytes 196616 | tf_op jit(solution)/shard_map/ppermute | solution.py:268
  25.2 0.9 %collective-permute-start.8 = (f32[2,32,256]{2,1,0:T(8,128)S(1)}, f32[2,32,256]{2,1,0:T(8,128)S(1)}, u32[]{:S(2)}, u32[]{:S(2)}) collective-permute-start(f32[2,32,256]{2,1,0:T(8,128)S(1)} %row_sweep.1.refs_0_), channel_id=1, source_target_pairs={{0,4},{4,0},{8,12},{12,8},{16,20},{20,16},{24,28},{28,24},{1,5},{5... | collective-permute-start | bytes 196616 | tf_op jit(solution)/shard_map/ppermute | solution.py:268
  26.1 1.5 %collective-permute-start.7 = (f32[2,32,256]{2,1,0:T(8,128)S(1)}, f32[2,32,256]{2,1,0:T(8,128)S(1)}, u32[]{:S(2)}, u32[]{:S(2)}) collective-permute-start(f32[2,32,256]{2,1,0:T(8,128)S(1)} %row_sweep.1.refs_0_), channel_id=1, source_target_pairs={{0,8},{4,12},{8,0},{12,4},{16,24},{20,28},{24,16},{28,20},{1,9},{5... | collective-permute-start | bytes 196616 | tf_op jit(solution)/shard_map/ppermute | solution.py:268
  27.5 1.7 %collective-permute-done.9.refs_3_ = f32[2,32,256]{2,1,0:T(8,128)S(1)} collective-permute-done((f32[2,32,256]{2,1,0:T(8,128)S(1)}, f32[2,32,256]{2,1,0:T(8,128)S(1)}, u32[]{:S(2)}, u32[]{:S(2)}) %collective-permute-start.9) | collective-permute-done | bytes 65568 | tf_op jit(solution)/shard_map/ppermute | solution.py:268
  29.2 0.7 %collective-permute-done.8.refs_2_ = f32[2,32,256]{2,1,0:T(8,128)S(1)} collective-permute-done((f32[2,32,256]{2,1,0:T(8,128)S(1)}, f32[2,32,256]{2,1,0:T(8,128)S(1)}, u32[]{:S(2)}, u32[]{:S(2)}) %collective-permute-start.8) | collective-permute-done | bytes 65568 | tf_op jit(solution)/shard_map/ppermute | solution.py:268
  29.9 0.4 %collective-permute-done.7.refs_1_ = f32[2,32,256]{2,1,0:T(8,128)S(1)} collective-permute-done((f32[2,32,256]{2,1,0:T(8,128)S(1)}, f32[2,32,256]{2,1,0:T(8,128)S(1)}, u32[]{:S(2)}, u32[]{:S(2)}) %collective-permute-start.7) | collective-permute-done | bytes 65568 | tf_op jit(solution)/shard_map/ppermute | solution.py:268
  30.3 0.8 %assemble.1 = f32[32,2048]{1,0:T(8,128)} custom-call(f32[2,32,256]{2,1,0:T(8,128)S(1)} %row_sweep.1.refs_0_, f32[2,32,256]{2,1,0:T(8,128)S(1)} %collective-permute-done.7.refs_1_, f32[2,32,256]{2,1,0:T(8,128)S(1)} %collective-permute-done.8.refs_2_, f32[2,32,256]{2,1,0:T(8,128)S(1)} %collective-permute-done.9.refs_3_), custom_call_target="tpu_custom_call" | custom-call | tf_op jit(solution)/shard_map/assemble/pallas_call | solution.py:19
  (1 shorter events, 0.0 us)
Async XLA Ops:
  0.0 7.5 %copy-start.1 = (f32[32,512]{1,0:T(8,128)S(1)}, f32[32,512]{1,0:T(8,128)}, u32[]{:S(2)}) copy-start(f32[32,512]{1,0:T(8,128)} %refs_0_.1) | copy-start | bytes 196612
  0.0 3.1 %collective-permute-start.2 = (f32[32,512]{1,0:T(8,128)}, f32[32,512]{1,0:T(8,128)S(1)}, u32[]{:S(2)}, u32[]{:S(2)}) collective-permute-start(f32[32,512]{1,0:T(8,128)} %refs_0_.1), channel_id=1, source_target_pairs={{0,1},{1,0},{2,3},{3,2},{4,5},{5,4},{6,7},{7,6},{8,9},{9,8},{10,11... | collective-permute-start | bytes 196616 | tf_op jit(solution)/shard_map/ppermute | solution.py:268
  0.5 6.4 %collective-permute-start.1 = (f32[32,512]{1,0:T(8,128)}, f32[32,512]{1,0:T(8,128)S(1)}, u32[]{:S(2)}, u32[]{:S(2)}) collective-permute-start(f32[32,512]{1,0:T(8,128)} %refs_0_.1), channel_id=1, source_target_pairs={{0,3},{1,2},{2,1},{3,0},{4,7},{5,6},{6,5},{7,4},{8,11},{9,10},{10,... | collective-permute-start | bytes 196616 | tf_op jit(solution)/shard_map/ppermute | solution.py:268
  3.1 4.5 %collective-permute-start = (f32[32,512]{1,0:T(8,128)}, f32[32,512]{1,0:T(8,128)S(1)}, u32[]{:S(2)}, u32[]{:S(2)}) collective-permute-start(f32[32,512]{1,0:T(8,128)} %refs_0_.1), channel_id=1, source_target_pairs={{0,2},{1,3},{2,0},{3,1},{4,6},{5,7},{6,4},{7,5},{8,10},{9,11},{10,... | collective-permute-start | bytes 196616 | tf_op jit(solution)/shard_map/ppermute | solution.py:268
  9.0 5.4 %collective-permute-start.3 = (f32[264,128]{1,0:T(8,128)S(1)}, f32[264,128]{1,0:T(8,128)S(1)}, u32[]{:S(2)}, u32[]{:S(2)}) collective-permute-start(f32[264,128]{1,0:T(8,128)S(1)} %get-tuple-element.24), channel_id=1, source_target_pairs={{0,4},{4,0},{8,12},{12,8},{16,20},{20,16},{24,28},{28,24},{1,5},{5... | collective-permute-start | bytes 405512 | tf_op jit(solution)/shard_map/ppermute | solution.py:268
  10.6 12.9 %copy-start = (f32[32,2048]{1,0:T(8,128)S(1)}, f32[32,2048]{1,0:T(8,128)}, u32[]{:S(2)}) copy-start(f32[32,2048]{1,0:T(8,128)} %refs_4_.1) | copy-start | bytes 786436
  14.4 5.5 %collective-permute-start.4 = (f32[136,128]{1,0:T(8,128)S(1)}, f32[136,128]{1,0:T(8,128)S(1)}, u32[]{:S(2)}, u32[]{:S(2)}) collective-permute-start(f32[136,128]{1,0:T(8,128)S(1)} %get-tuple-element.25), channel_id=1, source_target_pairs={{0,16},{4,20},{8,24},{12,28},{16,0},{20,4},{24,8},{28,12},{1,17},{... | collective-permute-start | bytes 208904 | tf_op jit(solution)/shard_map/ppermute | solution.py:268
  17.1 6.3 %collective-permute-start.5 = (f32[136,128]{1,0:T(8,128)S(1)}, f32[136,128]{1,0:T(8,128)S(1)}, u32[]{:S(2)}, u32[]{:S(2)}) collective-permute-start(f32[136,128]{1,0:T(8,128)S(1)} %get-tuple-element.26), channel_id=1, source_target_pairs={{0,24},{4,28},{8,16},{12,20},{16,8},{20,12},{24,0},{28,4},{1,25},{... | collective-permute-start | bytes 208904 | tf_op jit(solution)/shard_map/ppermute | solution.py:268
  18.4 5.1 %collective-permute-start.6 = (f32[136,128]{1,0:T(8,128)S(1)}, f32[136,128]{1,0:T(8,128)S(1)}, u32[]{:S(2)}, u32[]{:S(2)}) collective-permute-start(f32[136,128]{1,0:T(8,128)S(1)} %get-tuple-element.27), channel_id=1, source_target_pairs={{0,8},{4,12},{8,0},{12,4},{16,24},{20,28},{24,16},{28,20},{1,9},{5... | collective-permute-start | bytes 208904 | tf_op jit(solution)/shard_map/ppermute | solution.py:268
  24.0 5.3 %collective-permute-start.9 = (f32[2,32,256]{2,1,0:T(8,128)S(1)}, f32[2,32,256]{2,1,0:T(8,128)S(1)}, u32[]{:S(2)}, u32[]{:S(2)}) collective-permute-start(f32[2,32,256]{2,1,0:T(8,128)S(1)} %row_sweep.1.refs_0_), channel_id=1, source_target_pairs={{0,12},{4,8},{8,4},{12,0},{16,28},{20,24},{24,20},{28,16},{1,13},{... | collective-permute-start | bytes 196616 | tf_op jit(solution)/shard_map/ppermute | solution.py:268
  25.2 4.7 %collective-permute-start.8 = (f32[2,32,256]{2,1,0:T(8,128)S(1)}, f32[2,32,256]{2,1,0:T(8,128)S(1)}, u32[]{:S(2)}, u32[]{:S(2)}) collective-permute-start(f32[2,32,256]{2,1,0:T(8,128)S(1)} %row_sweep.1.refs_0_), channel_id=1, source_target_pairs={{0,4},{4,0},{8,12},{12,8},{16,20},{20,16},{24,28},{28,24},{1,5},{5... | collective-permute-start | bytes 196616 | tf_op jit(solution)/shard_map/ppermute | solution.py:268
  26.1 4.3 %collective-permute-start.7 = (f32[2,32,256]{2,1,0:T(8,128)S(1)}, f32[2,32,256]{2,1,0:T(8,128)S(1)}, u32[]{:S(2)}, u32[]{:S(2)}) collective-permute-start(f32[2,32,256]{2,1,0:T(8,128)S(1)} %row_sweep.1.refs_0_), channel_id=1, source_target_pairs={{0,8},{4,12},{8,0},{12,4},{16,24},{20,28},{24,16},{28,20},{1,9},{5... | collective-permute-start | bytes 196616 | tf_op jit(solution)/shard_map/ppermute | solution.py:268
where the time goes:
time: 31.2 us; the launch traced here: 31.1 us
  starting transfers between devices  12.5 us (40%)
  Pallas kernels  10.2 us (33%)
  waiting for transfers between devices  8.33 us (27%)
    ppermute x10, starting transfers between devices, permute(): return lax.ppermute(value, axis, [(i, i ^ turn) for i in range(size)])  12.5 us
    pallas_call x6, Pallas kernels, call(): pl.pallas_call(kernel, out_shape=out_shape, in_specs=in_specs or [VMEM] *...  10.2 us
    ppermute x10, waiting for transfers between devices, permute(): return lax.ppermute(value, axis, [(i, i ^ turn) for i in range(size)])  8.33 us
  transfers between devices with their start and end apart: 10, of which 7 were waited for; matrix products, arithmetic and copies ran while one was open for 0% of the time, Pallas kernels for 24%

commit v1 on v0

--- a/solution.py
+++ b/solution.py
@@ -223,14 +223,14 @@
     starts = [peer_start(near, width, at, side) for at in (level, level ^ 2)]
     h = jnp.concatenate([h_ref[:, pl.ds(start, width)] for start in starts], axis=1)
     rest = cross - exact_dot(gram, h, ((1,), (0,)))
-    rows = []
+    inverses = [1.0 / gram[k : k + 1, k : k + 1] for k in range(rank)]
+    steps = []
     for k in range(rank):
-        inverse = 1.0 / gram[k : k + 1, k : k + 1]
-        old = h[k : k + 1]
-        fresh = jnp.maximum(old + rest[k : k + 1] * inverse, 0.0)
-        rows.append(fresh)
-        rest = rest - gram[:, k : k + 1] * (fresh - old)
-    done = jnp.concatenate(rows, axis=0)
+        step = jnp.maximum(rest[k : k + 1] * inverses[k], -h[k : k + 1])
+        steps.append(step)
+        if k + 1 < rank:
+            rest = rest - gram[:, k : k + 1] * step
+    done = h + jnp.concatenate(steps, axis=0)
     for at in range(2):
         out_ref[at] = done[:, width * at : width * (at + 1)]
 

time: 31.2 us -> 31.2 us (level)
  no operation moved by 1% of the time
where the time goes in v1:
time: 31.2 us; the launch traced here: 31 us
  starting transfers between devices  12.5 us (40%)
  Pallas kernels  10.1 us (32%)
  waiting for transfers between devices  8.33 us (27%)
    ppermute x10, starting transfers between devices, permute(): return lax.ppermute(value, axis, [(i, i ^ turn) for i in range(size)])  12.5 us
    pallas_call x6, Pallas kernels, call(): pl.pallas_call(kernel, out_shape=out_shape, in_specs=in_specs or [VMEM] *...  10.1 us
    ppermute x10, waiting for transfers between devices, permute(): return lax.ppermute(value, axis, [(i, i ^ turn) for i in range(size)])  8.33 us
  transfers between devices with their start and end apart: 10, of which 7 were waited for; matrix products, arithmetic and copies ran while one was open for 0% of the time, Pallas kernels for 24%

profile of v1, /device:TPU:0, one launch (start us, length us, event | category | flops | bytes accessed | tf_op | source)
XLA Modules:
  0.0 31.0 jit_solution(7639132489792468017)
XLA Ops:
  0.0 0.0 copy-start.1
  0.0 0.5 %collective-permute-start.2 = (f32[32,512]{1,0:T(8,128)}, f32[32,512]{1,0:T(8,128)S(1)}, u32[]{:S(2)}, u32[]{:S(2)}) collective-permute-start(f32[32,512]{1,0:T(8,128)} %refs_0_.1), channel_id=1, source_target_pairs={{0,1},{1,0},{2,3},{3,2},{4,5},{5,4},{6,7},{7,6},{8,9},{9,8},{10,11... | collective-permute-start | bytes 196616 | tf_op jit(solution)/shard_map/ppermute | solution.py:268
  0.5 2.6 %collective-permute-start.1 = (f32[32,512]{1,0:T(8,128)}, f32[32,512]{1,0:T(8,128)S(1)}, u32[]{:S(2)}, u32[]{:S(2)}) collective-permute-start(f32[32,512]{1,0:T(8,128)} %refs_0_.1), channel_id=1, source_target_pairs={{0,3},{1,2},{2,1},{3,0},{4,7},{5,6},{6,5},{7,4},{8,11},{9,10},{10,... | collective-permute-start | bytes 196616 | tf_op jit(solution)/shard_map/ppermute | solution.py:268
  3.1 0.1 collective-permute-start
  3.1 0.0 collective-permute-done.2.refs_0_
  3.1 3.7 %load_other_side.1 = (f32[4,2048,256]{2,1,0:T(8,128)S(1)}, f32[4,64,128]{2,1,0:T(8,128)S(1)}, bf16[4,64,512]{2,1,0:T(8,128)(2,1)S(1)}, f32[32,32]{1,0:T(8,128)S(1)}) custom-call(f32[32,512]{1,0:T(8,128)S(1)} %collective-permute-done.2.refs_0_, f32[2048,2048]{1,0:T(8,128)} %data_ref.1), custom_call_target="tpu_custom_call" | custom-call | bytes 16777216 | tf_op jit(solution)/shard_map/load_other_side/pallas_call | solution.py:19
  6.8 0.0 collective-permute-done.1.refs_2_
  6.8 0.7 %collective-permute-done.refs_1_ = f32[32,512]{1,0:T(8,128)S(1)} collective-permute-done((f32[32,512]{1,0:T(8,128)}, f32[32,512]{1,0:T(8,128)S(1)}, u32[]{:S(2)}, u32[]{:S(2)}) %collective-permute-start) | collective-permute-done | bytes 65568 | tf_op jit(solution)/shard_map/ppermute | solution.py:268
  7.5 0.0 copy-done.1
  7.5 1.4 %other_side.1 = (f32[264,128]{1,0:T(8,128)S(1)}, bf16[4,64,512]{2,1,0:T(8,128)(2,1)S(1)}, f32[8,128]{1,0:T(8,128)S(1)}, f32[1,2048,256]{2,1,0:T(8,128)S(1)}) custom-call(f32[32,512]{1,0:T(8,128)S(1)} %copy-done.1, f32[32,512]{1,0:T(8,128)S(1)} %collective-permute-done.refs_1_, f32[32,512]{1,0:T(8,128)S(1)} %collective-permute-done.1.refs_2_, ...), custom_call_target="tpu_custom_call" | custom-call | tf_op jit(solution)/shard_map/other_side/pallas_call | solution.py:19
  9.0 1.6 %collective-permute-start.3 = (f32[264,128]{1,0:T(8,128)S(1)}, f32[264,128]{1,0:T(8,128)S(1)}, u32[]{:S(2)}, u32[]{:S(2)}) collective-permute-start(f32[264,128]{1,0:T(8,128)S(1)} %get-tuple-element.24), channel_id=1, source_target_pairs={{0,4},{4,0},{8,12},{12,8},{16,20},{20,16},{24,28},{28,24},{1,5},{5... | collective-permute-start | bytes 405512 | tf_op jit(solution)/shard_map/ppermute | solution.py:268
  10.6 0.0 copy-start
  10.6 3.8 %own_side.1.own_ref = f32[4,64,128]{2,1,0:T(8,128)S(1)} custom-call(bf16[4,64,512]{2,1,0:T(8,128)(2,1)S(1)} %get-tuple-element.21.w_split, f32[1,2048,256]{2,1,0:T(8,128)S(1)} %get-tuple-element.22.first_rows, f32[2048,2048]{1,0:T(8,128)} %data_ref.1), custom_call_target="tpu_custom_call" | custom-call | tf_op jit(solution)/shard_map/own_side/pallas_call | solution.py:19
  14.4 0.0 collective-permute-done.3.refs_0_
  14.4 2.7 %collective-permute-start.4 = (f32[136,128]{1,0:T(8,128)S(1)}, f32[136,128]{1,0:T(8,128)S(1)}, u32[]{:S(2)}, u32[]{:S(2)}) collective-permute-start(f32[136,128]{1,0:T(8,128)S(1)} %get-tuple-element.25), channel_id=1, source_target_pairs={{0,16},{4,20},{8,24},{12,28},{16,0},{20,4},{24,8},{28,12},{1,17},{... | collective-permute-start | bytes 208904 | tf_op jit(solution)/shard_map/ppermute | solution.py:268
  17.1 1.3 %collective-permute-start.5 = (f32[136,128]{1,0:T(8,128)S(1)}, f32[136,128]{1,0:T(8,128)S(1)}, u32[]{:S(2)}, u32[]{:S(2)}) collective-permute-start(f32[136,128]{1,0:T(8,128)S(1)} %get-tuple-element.26), channel_id=1, source_target_pairs={{0,24},{4,28},{8,16},{12,20},{16,8},{20,12},{24,0},{28,4},{1,25},{... | collective-permute-start | bytes 208904 | tf_op jit(solution)/shard_map/ppermute | solution.py:268
  18.4 0.2 collective-permute-start.6
  18.6 1.2 %collective-permute-done.4.refs_0_ = f32[136,128]{1,0:T(8,128)S(1)} collective-permute-done((f32[136,128]{1,0:T(8,128)S(1)}, f32[136,128]{1,0:T(8,128)S(1)}, u32[]{:S(2)}, u32[]{:S(2)}) %collective-permute-start.4) | collective-permute-done | bytes 69664 | tf_op jit(solution)/shard_map/ppermute | solution.py:268
  19.9 3.5 %collective-permute-done.5.refs_1_ = f32[136,128]{1,0:T(8,128)S(1)} collective-permute-done((f32[136,128]{1,0:T(8,128)S(1)}, f32[136,128]{1,0:T(8,128)S(1)}, u32[]{:S(2)}, u32[]{:S(2)}) %collective-permute-start.5) | collective-permute-done | bytes 69664 | tf_op jit(solution)/shard_map/ppermute | solution.py:268
  23.3 0.1 collective-permute-done.6.refs_2_
  23.5 0.0 copy-done
  23.5 0.4 %row_sweep.1.refs_0_ = f32[2,32,256]{2,1,0:T(8,128)S(1)} custom-call(f32[136,128]{1,0:T(8,128)S(1)} %collective-permute-done.4.refs_0_, f32[136,128]{1,0:T(8,128)S(1)} %collective-permute-done.5.refs_1_, f32[136,128]{1,0:T(8,128)S(1)} %collective-permute-done.6.refs_2_, f32[136,128]{1,0:T(8,128)S(1)} %get-tuple-element.28.refs_3_, f32[32,2048]{1,0:T(8,128)S(1)} %copy-done), custom_call_target="tpu_custom_call" | custom-call | tf_op jit(solution)/shard_map/row_sweep/pallas_call | solution.py:19
  23.9 1.2 %collective-permute-start.9 = (f32[2,32,256]{2,1,0:T(8,128)S(1)}, f32[2,32,256]{2,1,0:T(8,128)S(1)}, u32[]{:S(2)}, u32[]{:S(2)}) collective-permute-start(f32[2,32,256]{2,1,0:T(8,128)S(1)} %row_sweep.1.refs_0_), channel_id=1, source_target_pairs={{0,12},{4,8},{8,4},{12,0},{16,28},{20,24},{24,20},{28,16},{1,13},{... | collective-permute-start | bytes 196616 | tf_op jit(solution)/shard_map/ppermute | solution.py:268
  25.1 0.9 %collective-permute-start.8 = (f32[2,32,256]{2,1,0:T(8,128)S(1)}, f32[2,32,256]{2,1,0:T(8,128)S(1)}, u32[]{:S(2)}, u32[]{:S(2)}) collective-permute-start(f32[2,32,256]{2,1,0:T(8,128)S(1)} %row_sweep.1.refs_0_), channel_id=1, source_target_pairs={{0,4},{4,0},{8,12},{12,8},{16,20},{20,16},{24,28},{28,24},{1,5},{5... | collective-permute-start | bytes 196616 | tf_op jit(solution)/shard_map/ppermute | solution.py:268
  26.0 1.5 %collective-permute-start.7 = (f32[2,32,256]{2,1,0:T(8,128)S(1)}, f32[2,32,256]{2,1,0:T(8,128)S(1)}, u32[]{:S(2)}, u32[]{:S(2)}) collective-permute-start(f32[2,32,256]{2,1,0:T(8,128)S(1)} %row_sweep.1.refs_0_), channel_id=1, source_target_pairs={{0,8},{4,12},{8,0},{12,4},{16,24},{20,28},{24,16},{28,20},{1,9},{5... | collective-permute-start | bytes 196616 | tf_op jit(solution)/shard_map/ppermute | solution.py:268
  27.5 1.7 %collective-permute-done.9.refs_3_ = f32[2,32,256]{2,1,0:T(8,128)S(1)} collective-permute-done((f32[2,32,256]{2,1,0:T(8,128)S(1)}, f32[2,32,256]{2,1,0:T(8,128)S(1)}, u32[]{:S(2)}, u32[]{:S(2)}) %collective-permute-start.9) | collective-permute-done | bytes 65568 | tf_op jit(solution)/shard_map/ppermute | solution.py:268
  29.2 0.7 %collective-permute-done.8.refs_2_ = f32[2,32,256]{2,1,0:T(8,128)S(1)} collective-permute-done((f32[2,32,256]{2,1,0:T(8,128)S(1)}, f32[2,32,256]{2,1,0:T(8,128)S(1)}, u32[]{:S(2)}, u32[]{:S(2)}) %collective-permute-start.8) | collective-permute-done | bytes 65568 | tf_op jit(solution)/shard_map/ppermute | solution.py:268
  29.8 0.4 %collective-permute-done.7.refs_1_ = f32[2,32,256]{2,1,0:T(8,128)S(1)} collective-permute-done((f32[2,32,256]{2,1,0:T(8,128)S(1)}, f32[2,32,256]{2,1,0:T(8,128)S(1)}, u32[]{:S(2)}, u32[]{:S(2)}) %collective-permute-start.7) | collective-permute-done | bytes 65568 | tf_op jit(solution)/shard_map/ppermute | solution.py:268
  30.3 0.8 %assemble.1 = f32[32,2048]{1,0:T(8,128)} custom-call(f32[2,32,256]{2,1,0:T(8,128)S(1)} %row_sweep.1.refs_0_, f32[2,32,256]{2,1,0:T(8,128)S(1)} %collective-permute-done.7.refs_1_, f32[2,32,256]{2,1,0:T(8,128)S(1)} %collective-permute-done.8.refs_2_, f32[2,32,256]{2,1,0:T(8,128)S(1)} %collective-permute-done.9.refs_3_), custom_call_target="tpu_custom_call" | custom-call | tf_op jit(solution)/shard_map/assemble/pallas_call | solution.py:19
  (1 shorter events, 0.0 us)
Async XLA Ops:
  0.0 7.5 %copy-start.1 = (f32[32,512]{1,0:T(8,128)S(1)}, f32[32,512]{1,0:T(8,128)}, u32[]{:S(2)}) copy-start(f32[32,512]{1,0:T(8,128)} %refs_0_.1) | copy-start | bytes 196612
  0.0 3.1 %collective-permute-start.2 = (f32[32,512]{1,0:T(8,128)}, f32[32,512]{1,0:T(8,128)S(1)}, u32[]{:S(2)}, u32[]{:S(2)}) collective-permute-start(f32[32,512]{1,0:T(8,128)} %refs_0_.1), channel_id=1, source_target_pairs={{0,1},{1,0},{2,3},{3,2},{4,5},{5,4},{6,7},{7,6},{8,9},{9,8},{10,11... | collective-permute-start | bytes 196616 | tf_op jit(solution)/shard_map/ppermute | solution.py:268
  0.5 6.4 %collective-permute-start.1 = (f32[32,512]{1,0:T(8,128)}, f32[32,512]{1,0:T(8,128)S(1)}, u32[]{:S(2)}, u32[]{:S(2)}) collective-permute-start(f32[32,512]{1,0:T(8,128)} %refs_0_.1), channel_id=1, source_target_pairs={{0,3},{1,2},{2,1},{3,0},{4,7},{5,6},{6,5},{7,4},{8,11},{9,10},{10,... | collective-permute-start | bytes 196616 | tf_op jit(solution)/shard_map/ppermute | solution.py:268
  3.1 4.5 %collective-permute-start = (f32[32,512]{1,0:T(8,128)}, f32[32,512]{1,0:T(8,128)S(1)}, u32[]{:S(2)}, u32[]{:S(2)}) collective-permute-start(f32[32,512]{1,0:T(8,128)} %refs_0_.1), channel_id=1, source_target_pairs={{0,2},{1,3},{2,0},{3,1},{4,6},{5,7},{6,4},{7,5},{8,10},{9,11},{10,... | collective-permute-start | bytes 196616 | tf_op jit(solution)/shard_map/ppermute | solution.py:268
  9.0 5.4 %collective-permute-start.3 = (f32[264,128]{1,0:T(8,128)S(1)}, f32[264,128]{1,0:T(8,128)S(1)}, u32[]{:S(2)}, u32[]{:S(2)}) collective-permute-start(f32[264,128]{1,0:T(8,128)S(1)} %get-tuple-element.24), channel_id=1, source_target_pairs={{0,4},{4,0},{8,12},{12,8},{16,20},{20,16},{24,28},{28,24},{1,5},{5... | collective-permute-start | bytes 405512 | tf_op jit(solution)/shard_map/ppermute | solution.py:268
  10.6 12.9 %copy-start = (f32[32,2048]{1,0:T(8,128)S(1)}, f32[32,2048]{1,0:T(8,128)}, u32[]{:S(2)}) copy-start(f32[32,2048]{1,0:T(8,128)} %refs_4_.1) | copy-start | bytes 786436
  14.4 5.5 %collective-permute-start.4 = (f32[136,128]{1,0:T(8,128)S(1)}, f32[136,128]{1,0:T(8,128)S(1)}, u32[]{:S(2)}, u32[]{:S(2)}) collective-permute-start(f32[136,128]{1,0:T(8,128)S(1)} %get-tuple-element.25), channel_id=1, source_target_pairs={{0,16},{4,20},{8,24},{12,28},{16,0},{20,4},{24,8},{28,12},{1,17},{... | collective-permute-start | bytes 208904 | tf_op jit(solution)/shard_map/ppermute | solution.py:268
  17.1 6.3 %collective-permute-start.5 = (f32[136,128]{1,0:T(8,128)S(1)}, f32[136,128]{1,0:T(8,128)S(1)}, u32[]{:S(2)}, u32[]{:S(2)}) collective-permute-start(f32[136,128]{1,0:T(8,128)S(1)} %get-tuple-element.26), channel_id=1, source_target_pairs={{0,24},{4,28},{8,16},{12,20},{16,8},{20,12},{24,0},{28,4},{1,25},{... | collective-permute-start | bytes 208904 | tf_op jit(solution)/shard_map/ppermute | solution.py:268
  18.4 5.1 %collective-permute-start.6 = (f32[136,128]{1,0:T(8,128)S(1)}, f32[136,128]{1,0:T(8,128)S(1)}, u32[]{:S(2)}, u32[]{:S(2)}) collective-permute-start(f32[136,128]{1,0:T(8,128)S(1)} %get-tuple-element.27), channel_id=1, source_target_pairs={{0,8},{4,12},{8,0},{12,4},{16,24},{20,28},{24,16},{28,20},{1,9},{5... | collective-permute-start | bytes 208904 | tf_op jit(solution)/shard_map/ppermute | solution.py:268
  23.9 5.3 %collective-permute-start.9 = (f32[2,32,256]{2,1,0:T(8,128)S(1)}, f32[2,32,256]{2,1,0:T(8,128)S(1)}, u32[]{:S(2)}, u32[]{:S(2)}) collective-permute-start(f32[2,32,256]{2,1,0:T(8,128)S(1)} %row_sweep.1.refs_0_), channel_id=1, source_target_pairs={{0,12},{4,8},{8,4},{12,0},{16,28},{20,24},{24,20},{28,16},{1,13},{... | collective-permute-start | bytes 196616 | tf_op jit(solution)/shard_map/ppermute | solution.py:268
  25.1 4.7 %collective-permute-start.8 = (f32[2,32,256]{2,1,0:T(8,128)S(1)}, f32[2,32,256]{2,1,0:T(8,128)S(1)}, u32[]{:S(2)}, u32[]{:S(2)}) collective-permute-start(f32[2,32,256]{2,1,0:T(8,128)S(1)} %row_sweep.1.refs_0_), channel_id=1, source_target_pairs={{0,4},{4,0},{8,12},{12,8},{16,20},{20,16},{24,28},{28,24},{1,5},{5... | collective-permute-start | bytes 196616 | tf_op jit(solution)/shard_map/ppermute | solution.py:268
  26.0 4.3 %collective-permute-start.7 = (f32[2,32,256]{2,1,0:T(8,128)S(1)}, f32[2,32,256]{2,1,0:T(8,128)S(1)}, u32[]{:S(2)}, u32[]{:S(2)}) collective-permute-start(f32[2,32,256]{2,1,0:T(8,128)S(1)} %row_sweep.1.refs_0_), channel_id=1, source_target_pairs={{0,8},{4,12},{8,0},{12,4},{16,24},{20,28},{24,16},{28,20},{1,9},{5... | collective-permute-start | bytes 196616 | tf_op jit(solution)/shard_map/ppermute | solution.py:268

commit v2 on v1

--- a/solution.py
+++ b/solution.py
@@ -207,13 +207,10 @@
     side, level = lax.rem(row_at, near), lax.div(row_at, near)
     pieces = width // LANES
     slab = rank * pieces
-    packed, chunks = None, [None, None]
-    for part in parts:
-        gram_part = part[2 * slab :]
-        packed = gram_part if packed is None else packed + gram_part
-        for at in range(2):
-            piece = part[slab * at : slab * (at + 1)]
-            chunks[at] = piece if chunks[at] is None else chunks[at] + piece
+    two, three, one, own = (part[...] for part in parts)
+    total = (own + two) + (one + three)
+    packed = total[2 * slab :]
+    chunks = [total[slab * at : slab * (at + 1)] for at in range(2)]
     cross = jnp.concatenate(
         [chunk[rank * i : rank * (i + 1)] for chunk in chunks for i in range(pieces)], axis=1
     )

time: 31.2 us -> 31.2 us (level)
  no operation moved by 1% of the time
where the time goes in v2:
time: 31.2 us; the launch traced here: 31 us
  starting transfers between devices  12.5 us (40%)
  Pallas kernels  10.1 us (32%)
  waiting for transfers between devices  8.33 us (27%)
    ppermute x10, starting transfers between devices, permute(): return lax.ppermute(value, axis, [(i, i ^ turn) for i in range(size)])  12.5 us
    pallas_call x6, Pallas kernels, call(): pl.pallas_call(kernel, out_shape=out_shape, in_specs=in_specs or [VMEM] *...  10.1 us
    ppermute x10, waiting for transfers between devices, permute(): return lax.ppermute(value, axis, [(i, i ^ turn) for i in range(size)])  8.33 us
  transfers between devices with their start and end apart: 10, of which 7 were waited for; matrix products, arithmetic and copies ran while one was open for 0% of the time, Pallas kernels for 24%

profile of v2, /device:TPU:0, one launch (start us, length us, event | category | flops | bytes accessed | tf_op | source)
XLA Modules:
  0.0 31.0 jit_solution(7344267718554819238)
XLA Ops:
  0.0 0.0 copy-start.1
  0.0 0.5 %collective-permute-start.2 = (f32[32,512]{1,0:T(8,128)}, f32[32,512]{1,0:T(8,128)S(1)}, u32[]{:S(2)}, u32[]{:S(2)}) collective-permute-start(f32[32,512]{1,0:T(8,128)} %refs_0_.1), channel_id=1, source_target_pairs={{0,1},{1,0},{2,3},{3,2},{4,5},{5,4},{6,7},{7,6},{8,9},{9,8},{10,11... | collective-permute-start | bytes 196616 | tf_op jit(solution)/shard_map/ppermute | solution.py:265
  0.5 2.6 %collective-permute-start.1 = (f32[32,512]{1,0:T(8,128)}, f32[32,512]{1,0:T(8,128)S(1)}, u32[]{:S(2)}, u32[]{:S(2)}) collective-permute-start(f32[32,512]{1,0:T(8,128)} %refs_0_.1), channel_id=1, source_target_pairs={{0,3},{1,2},{2,1},{3,0},{4,7},{5,6},{6,5},{7,4},{8,11},{9,10},{10,... | collective-permute-start | bytes 196616 | tf_op jit(solution)/shard_map/ppermute | solution.py:265
  3.1 0.1 collective-permute-start
  3.1 0.0 collective-permute-done.2.refs_0_
  3.1 3.7 %load_other_side.1 = (f32[4,2048,256]{2,1,0:T(8,128)S(1)}, f32[4,64,128]{2,1,0:T(8,128)S(1)}, bf16[4,64,512]{2,1,0:T(8,128)(2,1)S(1)}, f32[32,32]{1,0:T(8,128)S(1)}) custom-call(f32[32,512]{1,0:T(8,128)S(1)} %collective-permute-done.2.refs_0_, f32[2048,2048]{1,0:T(8,128)} %data_ref.1), custom_call_target="tpu_custom_call" | custom-call | bytes 16777216 | tf_op jit(solution)/shard_map/load_other_side/pallas_call | solution.py:19
  6.8 0.0 collective-permute-done.1.refs_2_
  6.8 0.7 %collective-permute-done.refs_1_ = f32[32,512]{1,0:T(8,128)S(1)} collective-permute-done((f32[32,512]{1,0:T(8,128)}, f32[32,512]{1,0:T(8,128)S(1)}, u32[]{:S(2)}, u32[]{:S(2)}) %collective-permute-start) | collective-permute-done | bytes 65568 | tf_op jit(solution)/shard_map/ppermute | solution.py:265
  7.5 0.0 copy-done.1
  7.5 1.4 %other_side.1 = (f32[264,128]{1,0:T(8,128)S(1)}, bf16[4,64,512]{2,1,0:T(8,128)(2,1)S(1)}, f32[8,128]{1,0:T(8,128)S(1)}, f32[1,2048,256]{2,1,0:T(8,128)S(1)}) custom-call(f32[32,512]{1,0:T(8,128)S(1)} %copy-done.1, f32[32,512]{1,0:T(8,128)S(1)} %collective-permute-done.refs_1_, f32[32,512]{1,0:T(8,128)S(1)} %collective-permute-done.1.refs_2_, ...), custom_call_target="tpu_custom_call" | custom-call | tf_op jit(solution)/shard_map/other_side/pallas_call | solution.py:19
  9.0 1.6 %collective-permute-start.3 = (f32[264,128]{1,0:T(8,128)S(1)}, f32[264,128]{1,0:T(8,128)S(1)}, u32[]{:S(2)}, u32[]{:S(2)}) collective-permute-start(f32[264,128]{1,0:T(8,128)S(1)} %get-tuple-element.24), channel_id=1, source_target_pairs={{0,4},{4,0},{8,12},{12,8},{16,20},{20,16},{24,28},{28,24},{1,5},{5... | collective-permute-start | bytes 405512 | tf_op jit(solution)/shard_map/ppermute | solution.py:265
  10.6 0.0 copy-start
  10.6 3.8 %own_side.1.own_ref = f32[4,64,128]{2,1,0:T(8,128)S(1)} custom-call(bf16[4,64,512]{2,1,0:T(8,128)(2,1)S(1)} %get-tuple-element.21.w_split, f32[1,2048,256]{2,1,0:T(8,128)S(1)} %get-tuple-element.22.first_rows, f32[2048,2048]{1,0:T(8,128)} %data_ref.1), custom_call_target="tpu_custom_call" | custom-call | tf_op jit(solution)/shard_map/own_side/pallas_call | solution.py:19
  14.4 0.0 collective-permute-done.3.refs_0_
  14.4 2.7 %collective-permute-start.4 = (f32[136,128]{1,0:T(8,128)S(1)}, f32[136,128]{1,0:T(8,128)S(1)}, u32[]{:S(2)}, u32[]{:S(2)}) collective-permute-start(f32[136,128]{1,0:T(8,128)S(1)} %get-tuple-element.25), channel_id=1, source_target_pairs={{0,16},{4,20},{8,24},{12,28},{16,0},{20,4},{24,8},{28,12},{1,17},{... | collective-permute-start | bytes 208904 | tf_op jit(solution)/shard_map/ppermute | solution.py:265
  17.1 1.3 %collective-permute-start.5 = (f32[136,128]{1,0:T(8,128)S(1)}, f32[136,128]{1,0:T(8,128)S(1)}, u32[]{:S(2)}, u32[]{:S(2)}) collective-permute-start(f32[136,128]{1,0:T(8,128)S(1)} %get-tuple-element.26), channel_id=1, source_target_pairs={{0,24},{4,28},{8,16},{12,20},{16,8},{20,12},{24,0},{28,4},{1,25},{... | collective-permute-start | bytes 208904 | tf_op jit(solution)/shard_map/ppermute | solution.py:265
  18.4 0.2 collective-permute-start.6
  18.6 1.2 %collective-permute-done.4.refs_0_ = f32[136,128]{1,0:T(8,128)S(1)} collective-permute-done((f32[136,128]{1,0:T(8,128)S(1)}, f32[136,128]{1,0:T(8,128)S(1)}, u32[]{:S(2)}, u32[]{:S(2)}) %collective-permute-start.4) | collective-permute-done | bytes 69664 | tf_op jit(solution)/shard_map/ppermute | solution.py:265
  19.9 3.5 %collective-permute-done.5.refs_1_ = f32[136,128]{1,0:T(8,128)S(1)} collective-permute-done((f32[136,128]{1,0:T(8,128)S(1)}, f32[136,128]{1,0:T(8,128)S(1)}, u32[]{:S(2)}, u32[]{:S(2)}) %collective-permute-start.5) | collective-permute-done | bytes 69664 | tf_op jit(solution)/shard_map/ppermute | solution.py:265
  23.3 0.1 collective-permute-done.6.refs_2_
  23.5 0.0 copy-done
  23.5 0.4 %row_sweep.1.refs_0_ = f32[2,32,256]{2,1,0:T(8,128)S(1)} custom-call(f32[136,128]{1,0:T(8,128)S(1)} %collective-permute-done.4.refs_0_, f32[136,128]{1,0:T(8,128)S(1)} %collective-permute-done.5.refs_1_, f32[136,128]{1,0:T(8,128)S(1)} %collective-permute-done.6.refs_2_, f32[136,128]{1,0:T(8,128)S(1)} %get-tuple-element.28.refs_3_, f32[32,2048]{1,0:T(8,128)S(1)} %copy-done), custom_call_target="tpu_custom_call" | custom-call | tf_op jit(solution)/shard_map/row_sweep/pallas_call | solution.py:19
  23.9 1.2 %collective-permute-start.9 = (f32[2,32,256]{2,1,0:T(8,128)S(1)}, f32[2,32,256]{2,1,0:T(8,128)S(1)}, u32[]{:S(2)}, u32[]{:S(2)}) collective-permute-start(f32[2,32,256]{2,1,0:T(8,128)S(1)} %row_sweep.1.refs_0_), channel_id=1, source_target_pairs={{0,12},{4,8},{8,4},{12,0},{16,28},{20,24},{24,20},{28,16},{1,13},{... | collective-permute-start | bytes 196616 | tf_op jit(solution)/shard_map/ppermute | solution.py:265
  25.1 0.9 %collective-permute-start.8 = (f32[2,32,256]{2,1,0:T(8,128)S(1)}, f32[2,32,256]{2,1,0:T(8,128)S(1)}, u32[]{:S(2)}, u32[]{:S(2)}) collective-permute-start(f32[2,32,256]{2,1,0:T(8,128)S(1)} %row_sweep.1.refs_0_), channel_id=1, source_target_pairs={{0,4},{4,0},{8,12},{12,8},{16,20},{20,16},{24,28},{28,24},{1,5},{5... | collective-permute-start | bytes 196616 | tf_op jit(solution)/shard_map/ppermute | solution.py:265
  26.0 1.5 %collective-permute-start.7 = (f32[2,32,256]{2,1,0:T(8,128)S(1)}, f32[2,32,256]{2,1,0:T(8,128)S(1)}, u32[]{:S(2)}, u32[]{:S(2)}) collective-permute-start(f32[2,32,256]{2,1,0:T(8,128)S(1)} %row_sweep.1.refs_0_), channel_id=1, source_target_pairs={{0,8},{4,12},{8,0},{12,4},{16,24},{20,28},{24,16},{28,20},{1,9},{5... | collective-permute-start | bytes 196616 | tf_op jit(solution)/shard_map/ppermute | solution.py:265
  27.5 1.7 %collective-permute-done.9.refs_3_ = f32[2,32,256]{2,1,0:T(8,128)S(1)} collective-permute-done((f32[2,32,256]{2,1,0:T(8,128)S(1)}, f32[2,32,256]{2,1,0:T(8,128)S(1)}, u32[]{:S(2)}, u32[]{:S(2)}) %collective-permute-start.9) | collective-permute-done | bytes 65568 | tf_op jit(solution)/shard_map/ppermute | solution.py:265
  29.2 0.7 %collective-permute-done.8.refs_2_ = f32[2,32,256]{2,1,0:T(8,128)S(1)} collective-permute-done((f32[2,32,256]{2,1,0:T(8,128)S(1)}, f32[2,32,256]{2,1,0:T(8,128)S(1)}, u32[]{:S(2)}, u32[]{:S(2)}) %collective-permute-start.8) | collective-permute-done | bytes 65568 | tf_op jit(solution)/shard_map/ppermute | solution.py:265
  29.8 0.4 %collective-permute-done.7.refs_1_ = f32[2,32,256]{2,1,0:T(8,128)S(1)} collective-permute-done((f32[2,32,256]{2,1,0:T(8,128)S(1)}, f32[2,32,256]{2,1,0:T(8,128)S(1)}, u32[]{:S(2)}, u32[]{:S(2)}) %collective-permute-start.7) | collective-permute-done | bytes 65568 | tf_op jit(solution)/shard_map/ppermute | solution.py:265
  30.3 0.8 %assemble.1 = f32[32,2048]{1,0:T(8,128)} custom-call(f32[2,32,256]{2,1,0:T(8,128)S(1)} %row_sweep.1.refs_0_, f32[2,32,256]{2,1,0:T(8,128)S(1)} %collective-permute-done.7.refs_1_, f32[2,32,256]{2,1,0:T(8,128)S(1)} %collective-permute-done.8.refs_2_, f32[2,32,256]{2,1,0:T(8,128)S(1)} %collective-permute-done.9.refs_3_), custom_call_target="tpu_custom_call" | custom-call | tf_op jit(solution)/shard_map/assemble/pallas_call | solution.py:19
  (1 shorter events, 0.0 us)
Async XLA Ops:
  0.0 7.5 %copy-start.1 = (f32[32,512]{1,0:T(8,128)S(1)}, f32[32,512]{1,0:T(8,128)}, u32[]{:S(2)}) copy-start(f32[32,512]{1,0:T(8,128)} %refs_0_.1) | copy-start | bytes 196612
  0.0 3.1 %collective-permute-start.2 = (f32[32,512]{1,0:T(8,128)}, f32[32,512]{1,0:T(8,128)S(1)}, u32[]{:S(2)}, u32[]{:S(2)}) collective-permute-start(f32[32,512]{1,0:T(8,128)} %refs_0_.1), channel_id=1, source_target_pairs={{0,1},{1,0},{2,3},{3,2},{4,5},{5,4},{6,7},{7,6},{8,9},{9,8},{10,11... | collective-permute-start | bytes 196616 | tf_op jit(solution)/shard_map/ppermute | solution.py:265
  0.5 6.4 %collective-permute-start.1 = (f32[32,512]{1,0:T(8,128)}, f32[32,512]{1,0:T(8,128)S(1)}, u32[]{:S(2)}, u32[]{:S(2)}) collective-permute-start(f32[32,512]{1,0:T(8,128)} %refs_0_.1), channel_id=1, source_target_pairs={{0,3},{1,2},{2,1},{3,0},{4,7},{5,6},{6,5},{7,4},{8,11},{9,10},{10,... | collective-permute-start | bytes 196616 | tf_op jit(solution)/shard_map/ppermute | solution.py:265
  3.1 4.5 %collective-permute-start = (f32[32,512]{1,0:T(8,128)}, f32[32,512]{1,0:T(8,128)S(1)}, u32[]{:S(2)}, u32[]{:S(2)}) collective-permute-start(f32[32,512]{1,0:T(8,128)} %refs_0_.1), channel_id=1, source_target_pairs={{0,2},{1,3},{2,0},{3,1},{4,6},{5,7},{6,4},{7,5},{8,10},{9,11},{10,... | collective-permute-start | bytes 196616 | tf_op jit(solution)/shard_map/ppermute | solution.py:265
  9.0 5.4 %collective-permute-start.3 = (f32[264,128]{1,0:T(8,128)S(1)}, f32[264,128]{1,0:T(8,128)S(1)}, u32[]{:S(2)}, u32[]{:S(2)}) collective-permute-start(f32[264,128]{1,0:T(8,128)S(1)} %get-tuple-element.24), channel_id=1, source_target_pairs={{0,4},{4,0},{8,12},{12,8},{16,20},{20,16},{24,28},{28,24},{1,5},{5... | collective-permute-start | bytes 405512 | tf_op jit(solution)/shard_map/ppermute | solution.py:265
  10.6 12.9 %copy-start = (f32[32,2048]{1,0:T(8,128)S(1)}, f32[32,2048]{1,0:T(8,128)}, u32[]{:S(2)}) copy-start(f32[32,2048]{1,0:T(8,128)} %refs_4_.1) | copy-start | bytes 786436
  14.4 5.5 %collective-permute-start.4 = (f32[136,128]{1,0:T(8,128)S(1)}, f32[136,128]{1,0:T(8,128)S(1)}, u32[]{:S(2)}, u32[]{:S(2)}) collective-permute-start(f32[136,128]{1,0:T(8,128)S(1)} %get-tuple-element.25), channel_id=1, source_target_pairs={{0,16},{4,20},{8,24},{12,28},{16,0},{20,4},{24,8},{28,12},{1,17},{... | collective-permute-start | bytes 208904 | tf_op jit(solution)/shard_map/ppermute | solution.py:265
  17.1 6.3 %collective-permute-start.5 = (f32[136,128]{1,0:T(8,128)S(1)}, f32[136,128]{1,0:T(8,128)S(1)}, u32[]{:S(2)}, u32[]{:S(2)}) collective-permute-start(f32[136,128]{1,0:T(8,128)S(1)} %get-tuple-element.26), channel_id=1, source_target_pairs={{0,24},{4,28},{8,16},{12,20},{16,8},{20,12},{24,0},{28,4},{1,25},{... | collective-permute-start | bytes 208904 | tf_op jit(solution)/shard_map/ppermute | solution.py:265
  18.4 5.1 %collective-permute-start.6 = (f32[136,128]{1,0:T(8,128)S(1)}, f32[136,128]{1,0:T(8,128)S(1)}, u32[]{:S(2)}, u32[]{:S(2)}) collective-permute-start(f32[136,128]{1,0:T(8,128)S(1)} %get-tuple-element.27), channel_id=1, source_target_pairs={{0,8},{4,12},{8,0},{12,4},{16,24},{20,28},{24,16},{28,20},{1,9},{5... | collective-permute-start | bytes 208904 | tf_op jit(solution)/shard_map/ppermute | solution.py:265
  23.9 5.3 %collective-permute-start.9 = (f32[2,32,256]{2,1,0:T(8,128)S(1)}, f32[2,32,256]{2,1,0:T(8,128)S(1)}, u32[]{:S(2)}, u32[]{:S(2)}) collective-permute-start(f32[2,32,256]{2,1,0:T(8,128)S(1)} %row_sweep.1.refs_0_), channel_id=1, source_target_pairs={{0,12},{4,8},{8,4},{12,0},{16,28},{20,24},{24,20},{28,16},{1,13},{... | collective-permute-start | bytes 196616 | tf_op jit(solution)/shard_map/ppermute | solution.py:265
  25.1 4.7 %collective-permute-start.8 = (f32[2,32,256]{2,1,0:T(8,128)S(1)}, f32[2,32,256]{2,1,0:T(8,128)S(1)}, u32[]{:S(2)}, u32[]{:S(2)}) collective-permute-start(f32[2,32,256]{2,1,0:T(8,128)S(1)} %row_sweep.1.refs_0_), channel_id=1, source_target_pairs={{0,4},{4,0},{8,12},{12,8},{16,20},{20,16},{24,28},{28,24},{1,5},{5... | collective-permute-start | bytes 196616 | tf_op jit(solution)/shard_map/ppermute | solution.py:265
  26.0 4.3 %collective-permute-start.7 = (f32[2,32,256]{2,1,0:T(8,128)S(1)}, f32[2,32,256]{2,1,0:T(8,128)S(1)}, u32[]{:S(2)}, u32[]{:S(2)}) collective-permute-start(f32[2,32,256]{2,1,0:T(8,128)S(1)} %row_sweep.1.refs_0_), channel_id=1, source_target_pairs={{0,8},{4,12},{8,0},{12,4},{16,24},{20,28},{24,16},{28,20},{1,9},{5... | collective-permute-start | bytes 196616 | tf_op jit(solution)/shard_map/ppermute | solution.py:265

commit v3 on v2

--- a/solution.py
+++ b/solution.py
@@ -9,6 +9,7 @@
 
 LANES = 128
 GRAM_ROWS = 8
+LEVELS = 4
 VMEM = pl.BlockSpec(memory_space=pltpu.VMEM)
 HBM = pl.BlockSpec(memory_space=pltpu.HBM)
 
@@ -45,11 +46,14 @@
     )
 
 
+def peer_start(near, width, level, side):
+    return pl.multiple_of((side * LEVELS + level) * width, width)
+
+
 def block_start(near, width, side_turn, level_turn):
     row_at = lax.axis_index("prow")
     side, level = lax.rem(row_at, near), lax.div(row_at, near)
-    peer = (level ^ level_turn) * near + (side ^ side_turn)
-    return pl.multiple_of(peer * width, width)
+    return peer_start(near, width, level ^ level_turn, side ^ side_turn)
 
 
 def row_part(depth, turn):
@@ -196,10 +200,6 @@
         out_ref[slab * len(pair) :] = gram
 
 
-def peer_start(near, width, level, side):
-    return pl.multiple_of((level * near + side) * width, width)
-
-
 def sweep_kernel(near, width, *refs):
     parts, h_ref, out_ref = refs[:-2], refs[-2], refs[-1]
     rank = h_ref.shape[0]
@@ -254,7 +254,7 @@
     rank, depth = w_trans.shape
     rows, cols = data.shape
     width = cols // n_row
-    near = max(1, n_row // 4)
+    near = max(1, n_row // LEVELS)
     far = n_row // near
     slab = rank * (width // LANES)
     turns = [*range(far // 2, far), *range(far // 2 - 1, -1, -1)]

time: 31.2 us -> 31.1 us (level)
  no operation moved by 1% of the time
where the time goes in v3:
time: 31.1 us; the launch traced here: 31 us
  starting transfers between devices  12.5 us (40%)
  Pallas kernels  10 us (32%)
  waiting for transfers between devices  8.41 us (27%)
    ppermute x10, starting transfers between devices, permute(): return lax.ppermute(value, axis, [(i, i ^ turn) for i in range(size)])  12.5 us
    pallas_call x6, Pallas kernels, call(): pl.pallas_call(kernel, out_shape=out_shape, in_specs=in_specs or [VMEM] *...  10 us
    ppermute x10, waiting for transfers between devices, permute(): return lax.ppermute(value, axis, [(i, i ^ turn) for i in range(size)])  8.41 us
  transfers between devices with their start and end apart: 10, of which 7 were waited for; matrix products, arithmetic and copies ran while one was open for 0% of the time, Pallas kernels for 24%

profile of v3, /device:TPU:0, one launch (start us, length us, event | category | flops | bytes accessed | tf_op | source)
XLA Modules:
  0.0 31.0 jit_solution(14805037136616513228)
XLA Ops:
  0.0 0.0 copy-start.1
  0.0 0.5 %collective-permute-start.2 = (f32[32,512]{1,0:T(8,128)}, f32[32,512]{1,0:T(8,128)S(1)}, u32[]{:S(2)}, u32[]{:S(2)}) collective-permute-start(f32[32,512]{1,0:T(8,128)} %refs_0_.1), channel_id=1, source_target_pairs={{0,1},{1,0},{2,3},{3,2},{4,5},{5,4},{6,7},{7,6},{8,9},{9,8},{10,11... | collective-permute-start | bytes 196616 | tf_op jit(solution)/shard_map/ppermute | solution.py:265
  0.5 2.6 %collective-permute-start.1 = (f32[32,512]{1,0:T(8,128)}, f32[32,512]{1,0:T(8,128)S(1)}, u32[]{:S(2)}, u32[]{:S(2)}) collective-permute-start(f32[32,512]{1,0:T(8,128)} %refs_0_.1), channel_id=1, source_target_pairs={{0,3},{1,2},{2,1},{3,0},{4,7},{5,6},{6,5},{7,4},{8,11},{9,10},{10,... | collective-permute-start | bytes 196616 | tf_op jit(solution)/shard_map/ppermute | solution.py:265
  3.1 0.1 collective-permute-start
  3.1 0.0 collective-permute-done.2.refs_0_
  3.1 3.6 %load_other_side.1 = (f32[4,2048,256]{2,1,0:T(8,128)S(1)}, f32[4,64,128]{2,1,0:T(8,128)S(1)}, bf16[4,64,512]{2,1,0:T(8,128)(2,1)S(1)}, f32[32,32]{1,0:T(8,128)S(1)}) custom-call(f32[32,512]{1,0:T(8,128)S(1)} %collective-permute-done.2.refs_0_, f32[2048,2048]{1,0:T(8,128)} %data_ref.1), custom_call_target="tpu_custom_call" | custom-call | bytes 16777216 | tf_op jit(solution)/shard_map/load_other_side/pallas_call | solution.py:20
  6.7 0.0 collective-permute-done.1.refs_2_
  6.7 0.8 %collective-permute-done.refs_1_ = f32[32,512]{1,0:T(8,128)S(1)} collective-permute-done((f32[32,512]{1,0:T(8,128)}, f32[32,512]{1,0:T(8,128)S(1)}, u32[]{:S(2)}, u32[]{:S(2)}) %collective-permute-start) | collective-permute-done | bytes 65568 | tf_op jit(solution)/shard_map/ppermute | solution.py:265
  7.5 0.0 copy-done.1
  7.5 1.4 %other_side.1 = (f32[264,128]{1,0:T(8,128)S(1)}, bf16[4,64,512]{2,1,0:T(8,128)(2,1)S(1)}, f32[8,128]{1,0:T(8,128)S(1)}, f32[1,2048,256]{2,1,0:T(8,128)S(1)}) custom-call(f32[32,512]{1,0:T(8,128)S(1)} %copy-done.1, f32[32,512]{1,0:T(8,128)S(1)} %collective-permute-done.refs_1_, f32[32,512]{1,0:T(8,128)S(1)} %collective-permute-done.1.refs_2_, ...), custom_call_target="tpu_custom_call" | custom-call | tf_op jit(solution)/shard_map/other_side/pallas_call | solution.py:20
  9.0 1.6 %collective-permute-start.3 = (f32[264,128]{1,0:T(8,128)S(1)}, f32[264,128]{1,0:T(8,128)S(1)}, u32[]{:S(2)}, u32[]{:S(2)}) collective-permute-start(f32[264,128]{1,0:T(8,128)S(1)} %get-tuple-element.24), channel_id=1, source_target_pairs={{0,4},{4,0},{8,12},{12,8},{16,20},{20,16},{24,28},{28,24},{1,5},{5... | collective-permute-start | bytes 405512 | tf_op jit(solution)/shard_map/ppermute | solution.py:265
  10.6 0.0 copy-start
  10.6 3.8 %own_side.1.own_ref = f32[4,64,128]{2,1,0:T(8,128)S(1)} custom-call(bf16[4,64,512]{2,1,0:T(8,128)(2,1)S(1)} %get-tuple-element.21.w_split, f32[1,2048,256]{2,1,0:T(8,128)S(1)} %get-tuple-element.22.first_rows, f32[2048,2048]{1,0:T(8,128)} %data_ref.1), custom_call_target="tpu_custom_call" | custom-call | tf_op jit(solution)/shard_map/own_side/pallas_call | solution.py:20
  14.4 0.0 collective-permute-done.3.refs_0_
  14.4 2.7 %collective-permute-start.4 = (f32[136,128]{1,0:T(8,128)S(1)}, f32[136,128]{1,0:T(8,128)S(1)}, u32[]{:S(2)}, u32[]{:S(2)}) collective-permute-start(f32[136,128]{1,0:T(8,128)S(1)} %get-tuple-element.25), channel_id=1, source_target_pairs={{0,16},{4,20},{8,24},{12,28},{16,0},{20,4},{24,8},{28,12},{1,17},{... | collective-permute-start | bytes 208904 | tf_op jit(solution)/shard_map/ppermute | solution.py:265
  17.1 1.3 %collective-permute-start.5 = (f32[136,128]{1,0:T(8,128)S(1)}, f32[136,128]{1,0:T(8,128)S(1)}, u32[]{:S(2)}, u32[]{:S(2)}) collective-permute-start(f32[136,128]{1,0:T(8,128)S(1)} %get-tuple-element.26), channel_id=1, source_target_pairs={{0,24},{4,28},{8,16},{12,20},{16,8},{20,12},{24,0},{28,4},{1,25},{... | collective-permute-start | bytes 208904 | tf_op jit(solution)/shard_map/ppermute | solution.py:265
  18.4 0.2 collective-permute-start.6
  18.6 1.2 %collective-permute-done.4.refs_0_ = f32[136,128]{1,0:T(8,128)S(1)} collective-permute-done((f32[136,128]{1,0:T(8,128)S(1)}, f32[136,128]{1,0:T(8,128)S(1)}, u32[]{:S(2)}, u32[]{:S(2)}) %collective-permute-start.4) | collective-permute-done | bytes 69664 | tf_op jit(solution)/shard_map/ppermute | solution.py:265
  19.8 3.5 %collective-permute-done.5.refs_1_ = f32[136,128]{1,0:T(8,128)S(1)} collective-permute-done((f32[136,128]{1,0:T(8,128)S(1)}, f32[136,128]{1,0:T(8,128)S(1)}, u32[]{:S(2)}, u32[]{:S(2)}) %collective-permute-start.5) | collective-permute-done | bytes 69664 | tf_op jit(solution)/shard_map/ppermute | solution.py:265
  23.3 0.1 collective-permute-done.6.refs_2_
  23.5 0.0 copy-done
  23.5 0.4 %row_sweep.1.refs_0_ = f32[2,32,256]{2,1,0:T(8,128)S(1)} custom-call(f32[136,128]{1,0:T(8,128)S(1)} %collective-permute-done.4.refs_0_, f32[136,128]{1,0:T(8,128)S(1)} %collective-permute-done.5.refs_1_, f32[136,128]{1,0:T(8,128)S(1)} %collective-permute-done.6.refs_2_, f32[136,128]{1,0:T(8,128)S(1)} %get-tuple-element.28.refs_3_, f32[32,2048]{1,0:T(8,128)S(1)} %copy-done), custom_call_target="tpu_custom_call" | custom-call | tf_op jit(solution)/shard_map/row_sweep/pallas_call | solution.py:20
  23.9 1.2 %collective-permute-start.9 = (f32[2,32,256]{2,1,0:T(8,128)S(1)}, f32[2,32,256]{2,1,0:T(8,128)S(1)}, u32[]{:S(2)}, u32[]{:S(2)}) collective-permute-start(f32[2,32,256]{2,1,0:T(8,128)S(1)} %row_sweep.1.refs_0_), channel_id=1, source_target_pairs={{0,12},{4,8},{8,4},{12,0},{16,28},{20,24},{24,20},{28,16},{1,13},{... | collective-permute-start | bytes 196616 | tf_op jit(solution)/shard_map/ppermute | solution.py:265
  25.1 0.9 %collective-permute-start.8 = (f32[2,32,256]{2,1,0:T(8,128)S(1)}, f32[2,32,256]{2,1,0:T(8,128)S(1)}, u32[]{:S(2)}, u32[]{:S(2)}) collective-permute-start(f32[2,32,256]{2,1,0:T(8,128)S(1)} %row_sweep.1.refs_0_), channel_id=1, source_target_pairs={{0,4},{4,0},{8,12},{12,8},{16,20},{20,16},{24,28},{28,24},{1,5},{5... | collective-permute-start | bytes 196616 | tf_op jit(solution)/shard_map/ppermute | solution.py:265
  25.9 1.5 %collective-permute-start.7 = (f32[2,32,256]{2,1,0:T(8,128)S(1)}, f32[2,32,256]{2,1,0:T(8,128)S(1)}, u32[]{:S(2)}, u32[]{:S(2)}) collective-permute-start(f32[2,32,256]{2,1,0:T(8,128)S(1)} %row_sweep.1.refs_0_), channel_id=1, source_target_pairs={{0,8},{4,12},{8,0},{12,4},{16,24},{20,28},{24,16},{28,20},{1,9},{5... | collective-permute-start | bytes 196616 | tf_op jit(solution)/shard_map/ppermute | solution.py:265
  27.5 1.7 %collective-permute-done.9.refs_3_ = f32[2,32,256]{2,1,0:T(8,128)S(1)} collective-permute-done((f32[2,32,256]{2,1,0:T(8,128)S(1)}, f32[2,32,256]{2,1,0:T(8,128)S(1)}, u32[]{:S(2)}, u32[]{:S(2)}) %collective-permute-start.9) | collective-permute-done | bytes 65568 | tf_op jit(solution)/shard_map/ppermute | solution.py:265
  29.2 0.7 %collective-permute-done.8.refs_2_ = f32[2,32,256]{2,1,0:T(8,128)S(1)} collective-permute-done((f32[2,32,256]{2,1,0:T(8,128)S(1)}, f32[2,32,256]{2,1,0:T(8,128)S(1)}, u32[]{:S(2)}, u32[]{:S(2)}) %collective-permute-start.8) | collective-permute-done | bytes 65568 | tf_op jit(solution)/shard_map/ppermute | solution.py:265
  29.8 0.4 %collective-permute-done.7.refs_1_ = f32[2,32,256]{2,1,0:T(8,128)S(1)} collective-permute-done((f32[2,32,256]{2,1,0:T(8,128)S(1)}, f32[2,32,256]{2,1,0:T(8,128)S(1)}, u32[]{:S(2)}, u32[]{:S(2)}) %collective-permute-start.7) | collective-permute-done | bytes 65568 | tf_op jit(solution)/shard_map/ppermute | solution.py:265
  30.2 0.8 %assemble.1 = f32[32,2048]{1,0:T(8,128)} custom-call(f32[2,32,256]{2,1,0:T(8,128)S(1)} %row_sweep.1.refs_0_, f32[2,32,256]{2,1,0:T(8,128)S(1)} %collective-permute-done.7.refs_1_, f32[2,32,256]{2,1,0:T(8,128)S(1)} %collective-permute-done.8.refs_2_, f32[2,32,256]{2,1,0:T(8,128)S(1)} %collective-permute-done.9.refs_3_), custom_call_target="tpu_custom_call" | custom-call | tf_op jit(solution)/shard_map/assemble/pallas_call | solution.py:20
  (1 shorter events, 0.0 us)
Async XLA Ops:
  0.0 7.5 %copy-start.1 = (f32[32,512]{1,0:T(8,128)S(1)}, f32[32,512]{1,0:T(8,128)}, u32[]{:S(2)}) copy-start(f32[32,512]{1,0:T(8,128)} %refs_0_.1) | copy-start | bytes 196612
  0.0 3.1 %collective-permute-start.2 = (f32[32,512]{1,0:T(8,128)}, f32[32,512]{1,0:T(8,128)S(1)}, u32[]{:S(2)}, u32[]{:S(2)}) collective-permute-start(f32[32,512]{1,0:T(8,128)} %refs_0_.1), channel_id=1, source_target_pairs={{0,1},{1,0},{2,3},{3,2},{4,5},{5,4},{6,7},{7,6},{8,9},{9,8},{10,11... | collective-permute-start | bytes 196616 | tf_op jit(solution)/shard_map/ppermute | solution.py:265
  0.5 6.2 %collective-permute-start.1 = (f32[32,512]{1,0:T(8,128)}, f32[32,512]{1,0:T(8,128)S(1)}, u32[]{:S(2)}, u32[]{:S(2)}) collective-permute-start(f32[32,512]{1,0:T(8,128)} %refs_0_.1), channel_id=1, source_target_pairs={{0,3},{1,2},{2,1},{3,0},{4,7},{5,6},{6,5},{7,4},{8,11},{9,10},{10,... | collective-permute-start | bytes 196616 | tf_op jit(solution)/shard_map/ppermute | solution.py:265
  3.1 4.5 %collective-permute-start = (f32[32,512]{1,0:T(8,128)}, f32[32,512]{1,0:T(8,128)S(1)}, u32[]{:S(2)}, u32[]{:S(2)}) collective-permute-start(f32[32,512]{1,0:T(8,128)} %refs_0_.1), channel_id=1, source_target_pairs={{0,2},{1,3},{2,0},{3,1},{4,6},{5,7},{6,4},{7,5},{8,10},{9,11},{10,... | collective-permute-start | bytes 196616 | tf_op jit(solution)/shard_map/ppermute | solution.py:265
  9.0 5.4 %collective-permute-start.3 = (f32[264,128]{1,0:T(8,128)S(1)}, f32[264,128]{1,0:T(8,128)S(1)}, u32[]{:S(2)}, u32[]{:S(2)}) collective-permute-start(f32[264,128]{1,0:T(8,128)S(1)} %get-tuple-element.24), channel_id=1, source_target_pairs={{0,4},{4,0},{8,12},{12,8},{16,20},{20,16},{24,28},{28,24},{1,5},{5... | collective-permute-start | bytes 405512 | tf_op jit(solution)/shard_map/ppermute | solution.py:265
  10.6 12.9 %copy-start = (f32[32,2048]{1,0:T(8,128)S(1)}, f32[32,2048]{1,0:T(8,128)}, u32[]{:S(2)}) copy-start(f32[32,2048]{1,0:T(8,128)} %refs_4_.1) | copy-start | bytes 786436
  14.4 5.4 %collective-permute-start.4 = (f32[136,128]{1,0:T(8,128)S(1)}, f32[136,128]{1,0:T(8,128)S(1)}, u32[]{:S(2)}, u32[]{:S(2)}) collective-permute-start(f32[136,128]{1,0:T(8,128)S(1)} %get-tuple-element.25), channel_id=1, source_target_pairs={{0,16},{4,20},{8,24},{12,28},{16,0},{20,4},{24,8},{28,12},{1,17},{... | collective-permute-start | bytes 208904 | tf_op jit(solution)/shard_map/ppermute | solution.py:265
  17.1 6.3 %collective-permute-start.5 = (f32[136,128]{1,0:T(8,128)S(1)}, f32[136,128]{1,0:T(8,128)S(1)}, u32[]{:S(2)}, u32[]{:S(2)}) collective-permute-start(f32[136,128]{1,0:T(8,128)S(1)} %get-tuple-element.26), channel_id=1, source_target_pairs={{0,24},{4,28},{8,16},{12,20},{16,8},{20,12},{24,0},{28,4},{1,25},{... | collective-permute-start | bytes 208904 | tf_op jit(solution)/shard_map/ppermute | solution.py:265
  18.4 5.1 %collective-permute-start.6 = (f32[136,128]{1,0:T(8,128)S(1)}, f32[136,128]{1,0:T(8,128)S(1)}, u32[]{:S(2)}, u32[]{:S(2)}) collective-permute-start(f32[136,128]{1,0:T(8,128)S(1)} %get-tuple-element.27), channel_id=1, source_target_pairs={{0,8},{4,12},{8,0},{12,4},{16,24},{20,28},{24,16},{28,20},{1,9},{5... | collective-permute-start | bytes 208904 | tf_op jit(solution)/shard_map/ppermute | solution.py:265
  23.9 5.3 %collective-permute-start.9 = (f32[2,32,256]{2,1,0:T(8,128)S(1)}, f32[2,32,256]{2,1,0:T(8,128)S(1)}, u32[]{:S(2)}, u32[]{:S(2)}) collective-permute-start(f32[2,32,256]{2,1,0:T(8,128)S(1)} %row_sweep.1.refs_0_), channel_id=1, source_target_pairs={{0,12},{4,8},{8,4},{12,0},{16,28},{20,24},{24,20},{28,16},{1,13},{... | collective-permute-start | bytes 196616 | tf_op jit(solution)/shard_map/ppermute | solution.py:265
  25.1 4.8 %collective-permute-start.8 = (f32[2,32,256]{2,1,0:T(8,128)S(1)}, f32[2,32,256]{2,1,0:T(8,128)S(1)}, u32[]{:S(2)}, u32[]{:S(2)}) collective-permute-start(f32[2,32,256]{2,1,0:T(8,128)S(1)} %row_sweep.1.refs_0_), channel_id=1, source_target_pairs={{0,4},{4,0},{8,12},{12,8},{16,20},{20,16},{24,28},{28,24},{1,5},{5... | collective-permute-start | bytes 196616 | tf_op jit(solution)/shard_map/ppermute | solution.py:265
  25.9 4.3 %collective-permute-start.7 = (f32[2,32,256]{2,1,0:T(8,128)S(1)}, f32[2,32,256]{2,1,0:T(8,128)S(1)}, u32[]{:S(2)}, u32[]{:S(2)}) collective-permute-start(f32[2,32,256]{2,1,0:T(8,128)S(1)} %row_sweep.1.refs_0_), channel_id=1, source_target_pairs={{0,8},{4,12},{8,0},{12,4},{16,24},{20,28},{24,16},{28,20},{1,9},{5... | collective-permute-start | bytes 196616 | tf_op jit(solution)/shard_map/ppermute | solution.py:265
